TPU v7x, 512 devices: a whole 4x4x16 slice. The times are simulated.
512 devices in a mesh: pa: 4 (over x), mu: 32 (over y_lo, z), nu: 4 (over y_hi, core).
Axes of the slice: x: 4, y: 4 (y_hi: 2, y_lo: 2; y = y_hi * 2 + y_lo), z: 16, core: 2. Of those that a mesh axis runs over, the one named last changes fastest.
Arguments:
- integrals: bfloat16 [80, 1664, 1664], P('pa', 'mu', 'nu'), may hold values from -6 to 6
- pattern: int32 [128, 128], P('mu', 'nu'), may hold values 0 or 1
- occ_density: bfloat16 [1664, 1664], P(('mu', 'nu')), may hold values from -0.15625 to 0.15625
- virt_density: bfloat16 [1664, 1664], P(('mu', 'nu')), may hold values from -0.15625 to 0.15625
Outputs:
- chi: float32 [80, 80], P('pa')
Inputs may be any that keep to these rules, and one draw needn't show every extreme that they name: `pattern`: 0 or 1 for each pair of atoms.
All inputs are finite; a program needn't handle non-finite values. No bound on the sum of `pattern` on one device may be relied on, other than what follows from the above.
Results may differ from a plain program's by a relative error of at most 0.0042.
Values may be sent and summed in bfloat16 or wider, within the bound.
A program may use at most 64 MiB of HBM per device.

v0:
```python
import jax
import jax.numpy as jnp
from jax import lax
from jax.sharding import PartitionSpec as P


def local(integrals, pattern, occ_density, virt_density):
    slab, rows, cols = integrals.shape
    atom_rows, atom_cols = pattern.shape
    mu_count = lax.axis_size("mu")
    nu_count = lax.axis_size("nu")
    basis = rows * mu_count
    weights = pattern.astype(jnp.bfloat16)[None, :, None, :, None]
    shaped = integrals.reshape(slab, atom_rows, rows // atom_rows, atom_cols, cols // atom_cols)
    masked = (shaped * weights).reshape(slab, rows, cols)
    turned_block = jnp.transpose(masked, (2, 0, 1))
    scatter_across = lax.all_to_all(turned_block, "mu", split_axis=0, concat_axis=2, tiled=True)
    width = scatter_across.shape[0]

    def contract(fragment):
        return jnp.einsum(
            "dhv,vk->dhk", scatter_across, fragment, preferred_element_type=jnp.float32
        )

    occ_sum = contract(lax.all_gather(occ_density, ("mu", "nu"), axis=0, tiled=True))
    virt_sum = contract(lax.all_gather(virt_density, ("mu", "nu"), axis=0, tiled=True))
    occ_side = occ_sum.astype(jnp.bfloat16)
    parts = virt_sum.astype(jnp.bfloat16).reshape(width, slab, nu_count, mu_count, width)
    ordered = jnp.transpose(parts, (4, 3, 2, 0, 1))
    complete_input = ordered.reshape(width, mu_count * nu_count, width * slab)
    moved = lax.all_to_all(complete_input, ("mu", "nu"), split_axis=1, concat_axis=1, tiled=True)
    moved = moved.reshape(width, mu_count, nu_count, width, slab)
    turned = jnp.transpose(moved, (0, 4, 2, 1, 3)).reshape(width, slab, basis)
    block = jnp.einsum(
        "jpl,jql->pq",
        occ_side,
        lax.all_gather(turned, "pa", axis=1, tiled=True),
        preferred_element_type=jnp.float32,
    )
    summed = lax.psum(block, ("mu", "nu"))
    return summed / jnp.float32(basis)


def solution(mesh):
    placed = (P("pa", "mu", "nu"), P("mu", "nu"), P(("mu", "nu"), None), P(("mu", "nu"), None))
    return jax.shard_map(
        local, mesh=mesh, in_specs=placed, out_specs=P("pa", None), check_vma=False
    )
```

profile of v0, /device:TPU:1, one launch (start us, length us, event | category | flops | bytes accessed | tf_op | source)
XLA Modules:
  0.0 1074.4 jit_solution(5430435377636106843)
XLA Ops:
  6.5 0.0 all-gather.10.cloned.1.call-start
  6.5 0.7 all-gather.10.cloned.1.call-update
  7.3 0.0 all-gather.8.cloned.1.call-start
  7.3 0.7 all-gather.8.cloned.1.call-update
  8.0 0.0 all-gather.6.cloned.1.call-start
  8.1 3.2 copy.11
  11.3 0.7 convert_element_type.9
  12.0 0.1 mul.13
  12.1 0.6 mul.14
  12.7 0.1 copy.10
  12.9 1.7 multiply_bitcast_fusion
  14.6 5.0 reshape.31
  19.6 60.1 %all_to_all.23 = bf16[32,2,6760]{2,1,0:T(2,128)(2,1)S(1)} all-to-all(bf16[32,2,6760]{2,1,0:T(2,128)(2,1)S(1)} %reshape.31), channel_id=1, replica_groups=mesh['pa'=4,'mu'=32,'nu'=4] {'mu'}, dimensions={0} | all-to-all | bytes 1730560 | tf_op jit(solution)/shard_map/all_to_all | solution.py:17
  79.7 3.4 reshape.32
  83.1 1.7 copy.13
  84.8 4.7 all_to_all.19
  89.6 166.2 %all-gather.10.cloned.1.call-done = bf16[128,13,1664]{2,1,0:T(8,128)(2,1)} async-done(((bf16[1,13,1664]{2,1,0:T(8,128)(2,1)}), bf16[128,13,1664]{2,1,0:T(8,128)(2,1)}) %all-gather.10.cloned.1.call-update) | async-done | bytes 5537808 | tf_op jit(solution)/shard_map/all_gather | solution.py:26
  255.8 8.4 reshape.25
  264.2 4.8 convolution_convert_fusion
  269.0 23.6 %reshape.16 = bf16[13,20,4,32,13]{4,3,2,1,0:T(8,128)(2,1)} reshape(bf16[13,20,1664]{2,1,0:T(8,128)(2,1)S(1)} %convolution_convert_fusion) | data formatting | bytes 1730560 | tf_op jit(solution)/shard_map/reshape | solution.py:28
  292.6 19.4 %copy.22 = bf16[13,32,4,13,20]{4,3,0,2,1:T(8,128)(2,1)} copy(bf16[13,32,4,13,20]{0,1,2,4,3:T(8,128)(2,1)} %bitcast.26) | data formatting | bytes 1730560 | tf_op jit(solution)/shard_map/reshape | solution.py:30
  312.0 9.1 reshape.29
  321.1 100.2 %all_to_all.24 = bf16[13,128,260]{2,0,1:T(8,128)(2,1)S(1)} all-to-all(bf16[13,128,260]{2,0,1:T(8,128)(2,1)S(1)} %reshape.29), channel_id=1, replica_groups=mesh['pa'=4,'mu'=32,'nu'=4] {'mu','nu'}, dimensions={1} | all-to-all | bytes 1730560 | tf_op jit(solution)/shard_map/all_to_all | solution.py:31
  421.3 0.3 copy.16
  421.6 8.7 reshape.18
  430.3 22.7 %copy.23 = bf16[13,20,4,32,13]{4,3,2,0,1:T(8,128)(2,1)} copy(bf16[13,20,4,32,13]{1,4,2,3,0:T(8,128)(2,1)} %bitcast.27) | data formatting | bytes 1730560 | tf_op jit(solution)/shard_map/reshape | solution.py:33
  453.0 11.7 %reshape.30 = bf16[13,20,1664]{2,0,1:T(8,128)(2,1)} reshape(bf16[13,20,4,32,13]{4,3,2,0,1:T(8,128)(2,1)} %copy.23) | data formatting | bytes 1730560 | tf_op jit(solution)/shard_map/reshape | solution.py:33
  464.7 0.0 all-gather.6.cloned.1.call-update
  464.8 46.7 %all-gather.8.cloned.1.call-done = bf16[128,13,1664]{2,1,0:T(8,128)(2,1)} async-done(((bf16[1,13,1664]{2,1,0:T(8,128)(2,1)}), bf16[128,13,1664]{2,1,0:T(8,128)(2,1)}) %all-gather.8.cloned.1.call-update) | async-done | bytes 5537808 | tf_op jit(solution)/shard_map/all_gather | solution.py:25
  511.5 8.4 reshape.24
  519.9 46.4 %all-gather.6.cloned.1.call-done = bf16[13,80,1664]{2,0,1:T(8,128)(2,1)} async-done(((bf16[13,20,1664]{2,0,1:T(8,128)(2,1)}), bf16[13,80,1664]{2,0,1:T(8,128)(2,1)}) %all-gather.6.cloned.1.call-update) | async-done | bytes 3461136 | tf_op jit(solution)/shard_map/all_gather | solution.py:37
  566.3 8.6 fusion.2
  574.9 492.4 %psum.7 = f32[20,80]{1,0:T(8,128)S(1)} all-reduce(f32[20,80]{1,0:T(8,128)S(1)} %fusion.2), channel_id=1, replica_groups=mesh['pa'=4,'mu'=32,'nu'=4] {'mu','nu'}, use_global_device_ids=true, to_apply=%region_0.0 | all-reduce | flops 1600 | bytes 12800 | tf_op jit(solution)/shard_map/psum | solution.py:40
  1067.3 0.6 broadcast_multiply_fusion
Async XLA Ops:
  6.5 249.3 %all-gather.10.cloned.1.call-start = ((), (), s32[]{:S(2)}) async-start(), calls=%async_computation.4 | async-start | bytes 6868992 | tf_op jit(solution)/shard_map/all_gather | solution.py:26
  7.3 504.2 %all-gather.8.cloned.1.call-start = ((), (), s32[]{:S(2)}) async-start(), calls=%async_computation.3 | async-start | bytes 6868992 | tf_op jit(solution)/shard_map/all_gather | solution.py:25
  8.0 558.3 %all-gather.6.cloned.1.call-start = ((), (), s32[]{:S(2)}) async-start(), calls=%async_computation.2 | async-start | bytes 5324800 | tf_op jit(solution)/shard_map/all_gather | solution.py:37
Sparse Core Ops, SparseCore 0:
  9.5 246.2 all-gather.9
  258.0 253.4 all-gather.7
  513.6 52.7 all-gather.5
where the time goes:
time: 1090 us; the launch traced here: 1070 us
  blocking collectives  653 us (60%)
  waiting for transfers between devices  261 us (24%)
  local copies, waits for them, and re-layouts  131 us (12%)
  matrix products  13.3 us (1%)
  between operations  13.2 us (1%)
    psum x1, blocking collectives, local(): summed = lax.psum(block, ('mu', 'nu'))  492 us
    all_gather x1, waiting for transfers between devices, local(): lax.all_gather(virt_density, ('mu', 'nu'), axis=0, tiled=True)  166 us
    all_to_all x1, blocking collectives, local(): lax.all_to_all(complete_input, ('mu', 'nu'), split_axis=1, concat_axis=1,...  100 us
    all_to_all x1, blocking collectives, local(): lax.all_to_all(turned_block, 'mu', split_axis=0, concat_axis=2, tiled=True)  60.1 us
    all_gather x1, waiting for transfers between devices, local(): lax.all_gather(occ_density, ('mu', 'nu'), axis=0, tiled=True)  46.7 us
    all_gather x1, waiting for transfers between devices, local(): lax.all_gather(turned, 'pa', axis=1, tiled=True)  46.4 us
    reshape x2, local copies, waits for them, and re-layouts, local(): turned = jnp.transpose(moved, (0, 4, 2, 1, 3)).reshape(width, slab, basis)  34.5 us
    reshape x2, local copies, waits for them, and re-layouts, local(): complete_input = ordered.reshape(width, mu_count * nu_count, width * slab)  28.5 us
  transfers between devices with their start and end apart: 3, of which 3 were waited for; matrix products, arithmetic and copies ran while one was open for 12% of the time, Pallas kernels for 0%

commit v1 on v0

--- a/solution.py
+++ b/solution.py
@@ -1,7 +1,78 @@
+import functools
+
 import jax
 import jax.numpy as jnp
 from jax import lax
+from jax.experimental import pallas as pl
+from jax.experimental.pallas import tpu as pltpu
 from jax.sharding import PartitionSpec as P
+
+MESH = pl.DeviceIdType.MESH
+
+
+def groups():
+    pa, mu, nu = lax.axis_index("pa"), lax.axis_index("mu"), lax.axis_index("nu")
+    y_lo, z = mu // 16, mu % 16
+    plane = (8, y_lo * 4 + nu, lambda i: (pa, (i // 4) * 16 + z, i % 4))
+    near = (4, z % 4, lambda i: (pa, y_lo * 16 + (z // 4) * 4 + i, nu))
+    far = (4, z // 4, lambda i: (pa, y_lo * 16 + i * 4 + z % 4, nu))
+    return plane, near, far
+
+
+def sum_kernel(x_ref, o_ref, acc, got0, got1, got2, send_sem, recv_sem):
+    stages = groups()
+    barrier = pltpu.get_barrier_semaphore()
+    peers = 0
+    for size, me, at in stages:
+        for d in range(1, size):
+            pl.semaphore_signal(barrier, inc=1, device_id=at((me + d) % size), device_id_type=MESH)
+            peers += 1
+    acc[...] = x_ref[...]
+    pl.semaphore_wait(barrier, peers)
+    for s, ((size, me, at), got) in enumerate(zip(stages, (got0, got1, got2))):
+        copies = []
+        for d in range(1, size):
+            to = (me + d) % size
+            copy = pltpu.make_async_remote_copy(
+                src_ref=acc, dst_ref=got.at[me], send_sem=send_sem.at[s, d], recv_sem=recv_sem.at[s, me],
+                device_id=at(to), device_id_type=MESH)
+            copy.start()
+            copies.append(copy)
+        got[me] = acc[...]
+        for d in range(1, size):
+            frm = (me + d) % size
+            pltpu.make_async_remote_copy(
+                src_ref=acc, dst_ref=got.at[frm], send_sem=send_sem.at[s, d], recv_sem=recv_sem.at[s, frm],
+                device_id=at(frm), device_id_type=MESH).wait_recv()
+        total = got[0]
+        for i in range(1, size):
+            total = total + got[i]
+        for copy in copies:
+            copy.wait_send()
+        acc[...] = total
+    o_ref[...] = acc[...]
+
+
+def device_sum(block):
+    rows, cols = block.shape
+    padded = jnp.pad(block, ((0, -rows % 8), (0, -cols % 128)))
+    shape = padded.shape
+    summed = pl.pallas_call(
+        sum_kernel,
+        out_shape=jax.ShapeDtypeStruct(shape, jnp.float32),
+        in_specs=[pl.BlockSpec(memory_space=pltpu.VMEM)],
+        out_specs=pl.BlockSpec(memory_space=pltpu.VMEM),
+        scratch_shapes=[
+            pltpu.VMEM(shape, jnp.float32),
+            pltpu.VMEM((8,) + shape, jnp.float32),
+            pltpu.VMEM((4,) + shape, jnp.float32),
+            pltpu.VMEM((4,) + shape, jnp.float32),
+            pltpu.SemaphoreType.DMA((3, 8)),
+            pltpu.SemaphoreType.DMA((3, 8)),
+        ],
+        compiler_params=pltpu.CompilerParams(collective_id=0, has_side_effects=True),
+    )(padded)
+    return summed[:rows, :cols]
 
 
 def local(integrals, pattern, occ_density, virt_density):
@@ -37,7 +108,7 @@
         lax.all_gather(turned, "pa", axis=1, tiled=True),
         preferred_element_type=jnp.float32,
     )
-    summed = lax.psum(block, ("mu", "nu"))
+    summed = device_sum(block)
     return summed / jnp.float32(basis)
 
 

time: 1090 us -> 608 us (0.56); the launches traced: 1070 us -> 607 us
  blocking collectives: 653 us -> 160 us
  Pallas kernels: 0 us -> 24.4 us
    psum x1 -> x0, blocking collectives: 492 us -> none  [local(): summed = lax.psum(block, ('mu', 'nu'))]
    pallas_call x0 -> x1, Pallas kernels: none -> 24.4 us  [device_sum(): pl.pallas_call(sum_kernel, out_shape=jax.ShapeDtypeStruct(shape, jnp.floa...]
  transfers between devices with their start and end apart: 3 -> 3, of which waited for: 3 -> 3; matrix products, arithmetic and copies ran while one was open for 12% -> 22% of each run, Pallas kernels for 0% -> 0%
where the time goes in v1:
time: 608 us; the launch traced here: 607 us
  waiting for transfers between devices  260 us (43%)
  blocking collectives  160 us (26%)
  local copies, waits for them, and re-layouts  132 us (22%)
  Pallas kernels  24.4 us (4%)
  matrix products  13.3 us (2%)
  between operations  13.2 us (2%)
    all_gather x1, waiting for transfers between devices, local(): lax.all_gather(virt_density, ('mu', 'nu'), axis=0, tiled=True)  167 us
    all_to_all x1, blocking collectives, local(): lax.all_to_all(complete_input, ('mu', 'nu'), split_axis=1, concat_axis=1,...  99.9 us
    all_to_all x1, blocking collectives, local(): lax.all_to_all(turned_block, 'mu', split_axis=0, concat_axis=2, tiled=True)  60 us
    all_gather x1, waiting for transfers between devices, local(): lax.all_gather(turned, 'pa', axis=1, tiled=True)  47.6 us
    all_gather x1, waiting for transfers between devices, local(): lax.all_gather(occ_density, ('mu', 'nu'), axis=0, tiled=True)  44.4 us
    reshape x2, local copies, waits for them, and re-layouts, local(): turned = jnp.transpose(moved, (0, 4, 2, 1, 3)).reshape(width, slab, basis)  34.5 us
    reshape x2, local copies, waits for them, and re-layouts, local(): complete_input = ordered.reshape(width, mu_count * nu_count, width * slab)  28.5 us
    unnamed x5, local copies, waits for them, and re-layouts  28.4 us
  transfers between devices with their start and end apart: 3, of which 3 were waited for; matrix products, arithmetic and copies ran while one was open for 22% of the time, Pallas kernels for 0%

profile of v1, /device:TPU:1, one launch (start us, length us, event | category | flops | bytes accessed | tf_op | source)
XLA Modules:
  0.0 606.9 jit_solution(17495275358617322184)
XLA Ops:
  6.5 0.0 all-gather.10.cloned.1.call-start
  6.5 0.7 all-gather.10.cloned.1.call-update
  7.3 0.0 all-gather.8.cloned.1.call-start
  7.3 0.7 all-gather.8.cloned.1.call-update
  8.0 0.0 all-gather.6.cloned.1.call-start
  8.1 3.2 copy.11
  11.3 0.7 convert_element_type.11
  12.0 0.1 mul.13
  12.1 0.6 mul.14
  12.7 0.1 copy.10
  12.9 1.7 multiply_bitcast_fusion
  14.6 5.0 reshape.31
  19.6 60.0 %all_to_all.23 = bf16[32,2,6760]{2,1,0:T(2,128)(2,1)S(1)} all-to-all(bf16[32,2,6760]{2,1,0:T(2,128)(2,1)S(1)} %reshape.31), channel_id=1, replica_groups=mesh['pa'=4,'mu'=32,'nu'=4] {'mu'}, dimensions={0} | all-to-all | bytes 1730560 | tf_op jit(solution)/shard_map/all_to_all | solution.py:88
  79.6 3.4 reshape.32
  83.0 1.7 copy.13
  84.7 4.8 all_to_all.19
  89.5 166.9 %all-gather.10.cloned.1.call-done = bf16[128,13,1664]{2,1,0:T(8,128)(2,1)} async-done(((bf16[1,13,1664]{2,1,0:T(8,128)(2,1)}), bf16[128,13,1664]{2,1,0:T(8,128)(2,1)}) %all-gather.10.cloned.1.call-update) | async-done | bytes 5537808 | tf_op jit(solution)/shard_map/all_gather | solution.py:97
  256.4 8.4 %reshape.25 = bf16[1664,1664,1]{1,0,2:T(8,128)(2,1)} reshape(bf16[128,13,1664]{2,1,0:T(8,128)(2,1)} %all-gather.10.cloned.1.call-done) | data formatting | bytes 11075584
  264.7 4.8 convolution_convert_fusion
  269.5 23.6 %reshape.16 = bf16[13,20,4,32,13]{4,3,2,1,0:T(8,128)(2,1)} reshape(bf16[13,20,1664]{2,1,0:T(8,128)(2,1)S(1)} %convolution_convert_fusion) | data formatting | bytes 1730560 | tf_op jit(solution)/shard_map/reshape | solution.py:99
  293.1 19.5 %copy.22 = bf16[13,32,4,13,20]{4,3,0,2,1:T(8,128)(2,1)} copy(bf16[13,32,4,13,20]{0,1,2,4,3:T(8,128)(2,1)} %bitcast.26) | data formatting | bytes 1730560 | tf_op jit(solution)/shard_map/reshape | solution.py:101
  312.6 9.1 %reshape.29 = bf16[13,128,260]{2,0,1:T(8,128)(2,1)S(1)} reshape(bf16[13,32,4,13,20]{4,3,0,2,1:T(8,128)(2,1)} %copy.22) | data formatting | bytes 1730560 | tf_op jit(solution)/shard_map/reshape | solution.py:101
  321.7 99.9 %all_to_all.24 = bf16[13,128,260]{2,0,1:T(8,128)(2,1)S(1)} all-to-all(bf16[13,128,260]{2,0,1:T(8,128)(2,1)S(1)} %reshape.29), channel_id=1, replica_groups=mesh['pa'=4,'mu'=32,'nu'=4] {'mu','nu'}, dimensions={1} | all-to-all | bytes 1730560 | tf_op jit(solution)/shard_map/all_to_all | solution.py:102
  421.6 0.3 copy.16
  421.9 8.7 %reshape.18 = bf16[13,32,4,13,20]{4,3,2,1,0:T(8,128)(2,1)} reshape(bf16[13,128,260]{2,1,0:T(8,128)(2,1)S(1)} %copy.16) | data formatting | bytes 1730560 | tf_op jit(solution)/shard_map/reshape | solution.py:103
  430.6 22.7 %copy.23 = bf16[13,20,4,32,13]{4,3,2,0,1:T(8,128)(2,1)} copy(bf16[13,20,4,32,13]{1,4,2,3,0:T(8,128)(2,1)} %bitcast.27) | data formatting | bytes 1730560 | tf_op jit(solution)/shard_map/reshape | solution.py:104
  453.3 11.8 %reshape.30 = bf16[13,20,1664]{2,0,1:T(8,128)(2,1)} reshape(bf16[13,20,4,32,13]{4,3,2,0,1:T(8,128)(2,1)} %copy.23) | data formatting | bytes 1730560 | tf_op jit(solution)/shard_map/reshape | solution.py:104
  465.1 0.0 all-gather.6.cloned.1.call-update
  465.1 44.4 %all-gather.8.cloned.1.call-done = bf16[128,13,1664]{2,1,0:T(8,128)(2,1)} async-done(((bf16[1,13,1664]{2,1,0:T(8,128)(2,1)}), bf16[128,13,1664]{2,1,0:T(8,128)(2,1)}) %all-gather.8.cloned.1.call-update) | async-done | bytes 5537808 | tf_op jit(solution)/shard_map/all_gather | solution.py:96
  509.5 8.4 %reshape.24 = bf16[1664,1664,1]{1,0,2:T(8,128)(2,1)} reshape(bf16[128,13,1664]{2,1,0:T(8,128)(2,1)} %all-gather.8.cloned.1.call-done) | data formatting | bytes 11075584
  517.9 47.6 %all-gather.6.cloned.1.call-done = bf16[13,80,1664]{2,0,1:T(8,128)(2,1)} async-done(((bf16[13,20,1664]{2,0,1:T(8,128)(2,1)}), bf16[13,80,1664]{2,0,1:T(8,128)(2,1)}) %all-gather.6.cloned.1.call-update) | async-done | bytes 3461136 | tf_op jit(solution)/shard_map/all_gather | solution.py:108
  565.4 8.6 %fusion.2 = f32[20,80]{1,0:T(8,128)S(1)} fusion(bf16[13,80,1664]{2,0,1:T(8,128)(2,1)} %all-gather.6.cloned.1.call-done, bf16[13,20,1664]{2,1,0:T(8,128)(2,1)S(1)} %all_to_all.19, bf16[1664,1664,1]{1,0,2:T(8,128)(2,1)} %reshape.24), kind=kOutput, calls=%fused_computation.5 | convolution fusion | flops 1509480960 | bytes 9870592 | tf_op jit(solution)/shard_map/jpl,jql->pq/dot_general | solution.py:105
  574.0 0.6 pad.4.x_ref
  574.6 24.4 %shard_map.46 = f32[24,128]{1,0:T(8,128)} custom-call(f32[24,128]{1,0:T(8,128)} %pad.4.x_ref), custom_call_target="tpu_custom_call" | custom-call | tf_op jit(solution)/shard_map/pallas_call | solution.py:60
  599.0 1.3 slice_multiply_fusion
Async XLA Ops:
  6.5 249.8 %all-gather.10.cloned.1.call-start = ((), (), s32[]{:S(2)}) async-start(), calls=%async_computation.4 | async-start | bytes 6868992 | tf_op jit(solution)/shard_map/all_gather | solution.py:97
  7.3 502.2 %all-gather.8.cloned.1.call-start = ((), (), s32[]{:S(2)}) async-start(), calls=%async_computation.3 | async-start | bytes 6868992 | tf_op jit(solution)/shard_map/all_gather | solution.py:96
  8.0 557.4 %all-gather.6.cloned.1.call-start = ((), (), s32[]{:S(2)}) async-start(), calls=%async_computation.2 | async-start | bytes 5324800 | tf_op jit(solution)/shard_map/all_gather | solution.py:108
Sparse Core Ops, SparseCore 0:
  9.5 246.8 all-gather.9
  258.5 250.8 all-gather.7
  511.6 53.8 all-gather.5

commit v2 on v0

v2 whole, which is shorter than its diff:
```python
import functools

import jax
import jax.numpy as jnp
from jax import lax
from jax.experimental import pallas as pl
from jax.experimental.pallas import tpu as pltpu
from jax.sharding import PartitionSpec as P

MESH = pl.DeviceIdType.MESH
F32, BF16 = jnp.float32, jnp.bfloat16
PA, MU, NU, DEEP = 4, 32, 4, 16
BAS, TALL = 13, 16
SLAB, ROWS, COLS = 20, 52, 416
RI = PA * SLAB
CHUNKS = COLS // TALL
HALF = CHUNKS // 2
WIDE = 1152
SIDE = 512
LINES = RI * TALL
DEPTH = MU * NU * TALL
BLOCK = 24
VMEM = pl.BlockSpec(memory_space=pltpu.VMEM)
LIMIT = 56 * 1024 * 1024


def nt(a, b):
    return lax.dot_general(a, b, (((1,), (1,)), ((), ())), preferred_element_type=F32)


def nn(a, b):
    return jnp.dot(a, b, preferred_element_type=F32)


def iotas(shape):
    return lax.broadcasted_iota(jnp.int32, shape, 0), lax.broadcasted_iota(jnp.int32, shape, 1)


def one_hot(where):
    return jnp.where(where, 1.0, 0.0).astype(BF16)


def place():
    pa, mu, nu = lax.axis_index("pa"), lax.axis_index("mu"), lax.axis_index("nu")
    z = mu % DEEP
    return pa, mu, nu, z % 5 != 4, (mu // DEEP) * HALF + z - z // 5


def chunk_mu(chunk):
    r = chunk % HALF
    return (chunk // HALF) * DEEP + r + r // 4


def remote(src, dst, send, recv, device):
    return pltpu.make_async_remote_copy(
        src_ref=src, dst_ref=dst, send_sem=send, recv_sem=recv, device_id=device, device_id_type=MESH)


def turn_kernel(m_ref, pat_ref, o_ref, held):
    r, c = iotas((64, 4))
    spread_m = one_hot(((r >= c * BAS) & (r < c * BAS + BAS)))
    r, c = iotas((32, COLS))
    spread_n = one_hot(((c >= r * BAS) & (c < r * BAS + BAS)))
    pat = nn(spread_m, pat_ref[...].astype(F32).astype(BF16))
    mask = nn(pat.astype(BF16), spread_n)[:ROWS]
    held[...] = jnp.zeros_like(held)
    for p in range(SLAB):
        held[p, :ROWS, :] = (m_ref[p].astype(F32) * mask).astype(BF16)
    r, c = iotas((WIDE, 256))
    eye_r, eye_c = iotas((COLS, COLS))
    eye = one_hot(eye_r == eye_c)
    dense = jnp.zeros((WIDE, COLS), F32)
    for g in range(SLAB // 4):
        p, m = 4 * g + c // 64, c % 64
        pick = one_hot((r == p * ROWS + m) & (m < ROWS))
        dense = dense + nn(pick, held[4 * g:4 * g + 4].reshape(256, COLS))
    o_ref[...] = nt(eye, dense.astype(BF16)).astype(BF16)


def turn(integrals, pattern):
    return pl.pallas_call(
        turn_kernel,
        out_shape=jax.ShapeDtypeStruct((COLS, WIDE), BF16),
        in_specs=[VMEM, VMEM],
        out_specs=VMEM,
        scratch_shapes=[pltpu.VMEM((SLAB, 64, COLS), BF16)],
        compiler_params=pltpu.CompilerParams(vmem_limit_bytes=LIMIT),
    )(integrals, pattern)


def spread_kernel(b_ref, d_ref, got, den, mu_send, fwd_send, got_recv, own_sem, far_send, far_recv, near_send, near_recv,
                  y_send, y_recv, core_send, core_recv):
    pa, mu, nu, works, chunk = place()
    y_lo, z, y_hi, core = mu // DEEP, mu % DEEP, nu // 2, nu % 2
    zh, zl = z // 4, z % 4
    y = y_hi * 2 + y_lo

    def at_y(other):
        return (pa, (other % 2) * DEEP + z, (other // 2) * 2 + core)

    mate = (pa, mu, y_hi * 2 + 1 - core)
    barrier = pltpu.get_barrier_semaphore()

    def greet(device):
        pl.semaphore_signal(barrier, inc=1, device_id=device, device_id_type=MESH)

    @pl.loop(1, MU)
    def _(d):
        greet((pa, (mu + d) % MU, nu))

    for d in range(1, PA):
        greet(((pa + d) % PA, mu, nu))
    greet((pa, mu, (1 - y_hi) * 2 + core))
    greet((pa, (1 - y_lo) * DEEP + z, (1 - y_hi) * 2 + core))
    greet(mate)
    den[mu, nu] = d_ref[...]
    pl.semaphore_wait(barrier, MU - 1 + PA - 1 + 3)

    def far(i, s):
        return remote(den.at[mu, nu], den.at[mu, nu], far_send.at[s], far_recv.at[zh], (pa, y_lo * DEEP + i * 4 + zl, nu))

    for d in range(1, 4):
        far((zh + d) % 4, d).start()

    def across(d):
        j = (chunk + d) % CHUNKS
        src = b_ref.at[pl.ds(pl.multiple_of(j * TALL, TALL), TALL), :]
        return src, remote(src, got.at[pa, mu], mu_send.at[d], got_recv.at[pa, mu], (pa, chunk_mu(j), nu))

    @pl.when(works)
    def _():
        pltpu.make_async_copy(across(0)[0], got.at[pa, mu], own_sem).start()

    @pl.when(jnp.logical_not(works))
    def _():
        across(0)[1].start()

    @pl.loop(1, CHUNKS)
    def _(d):
        across(d)[1].start()

    def far_got(i):
        src = den.at[y_lo * DEEP + i * 4 + zl, nu]
        return remote(src, src, far_send.at[0], far_recv.at[i], mate)

    def near(i, h, s):
        src = den.at[y_lo * DEEP + h * 4 + zl, nu]
        return remote(src, src, near_send.at[s, h], near_recv.at[zl, h], (pa, y_lo * DEEP + zh * 4 + i, nu))

    def near_got(i, h):
        src = den.at[y_lo * DEEP + h * 4 + i, nu]
        return remote(src, src, near_send.at[0, 0], near_recv.at[i, h], mate)

    for d in range(1, 4):
        near((zl + d) % 4, zh, d).start()
    for e in range(1, 4):
        h = (zh + e) % 4
        far_got(h).wait_recv()
        for d in range(1, 4):
            near((zl + d) % 4, h, d).start()

    def slot(x, k):
        return remote(got.at[x, k], got.at[x, k], mu_send.at[0], got_recv.at[x, k], mate)

    def forward(k, d):
        return remote(got.at[pa, k], got.at[pa, k], fwd_send.at[k, d], got_recv.at[pa, k], ((pa + d) % PA, mu, nu))

    def pass_on(low, high):
        @pl.when(works)
        def _():
            @pl.loop(low, high)
            def _(e):
                k = (mu + MU - e) % MU
                slot(pa, k).wait_recv()
                for d in range(1, PA):
                    forward(k, d).start()

    @pl.when(works)
    def _():
        pltpu.make_async_copy(across(0)[0], got.at[pa, mu], own_sem).wait()
        for d in range(1, PA):
            forward(mu, d).start()

    pass_on(1, 8)

    for d in range(1, 4):
        for h in range(4):
            near_got((zl + d) % 4, h).wait_recv()

    def plane(other):
        return den.at[pl.ds((other % 2) * DEEP, DEEP), (other // 2) * 2 + core]

    def over_y(d):
        return remote(plane(y), plane(y), y_send.at[d], y_recv.at[y], at_y((y + d) % 4))

    def y_got(other):
        return remote(plane(other), plane(other), y_send.at[0], y_recv.at[other], mate)

    def to_mate(other):
        return remote(plane(other), plane(other), core_send.at[other], core_recv.at[other], mate)

    def mate_got(other):
        theirs = den.at[pl.ds((other % 2) * DEEP, DEEP), (other // 2) * 2 + 1 - core]
        return remote(theirs, theirs, core_send.at[0], core_recv.at[other], mate)

    for d in range(1, 4):
        over_y(d).start()
    to_mate(y).start()
    pass_on(8, 20)
    for d in range(1, 4):
        y_got((y + d) % 4).wait_recv()
        to_mate((y + d) % 4).start()
    pass_on(20, MU)

    @pl.when(works)
    def _():
        for d in range(1, PA):
            @pl.loop(0, MU)
            def _(k):
                slot((pa + d) % PA, k).wait_recv()

        @pl.loop(0, MU)
        def _(k):
            for d in range(1, PA):
                forward(k, d).wait_send()

    for other in range(4):
        mate_got(other).wait_recv()
        to_mate(other).wait_send()
    for d in range(1, 4):
        over_y(d).wait_send()
        far((zh + d) % 4, d).wait_send()
        for h in range(4):
            near((zl + d) % 4, h, d).wait_send()

    @pl.when(jnp.logical_not(works))
    def _():
        across(0)[1].wait_send()

    @pl.loop(1, CHUNKS)
    def _(d):
        across(d)[1].wait_send()


def spread(block, density):
    dma = pltpu.SemaphoreType.DMA
    return pl.pallas_call(
        spread_kernel,
        out_shape=(jax.ShapeDtypeStruct((PA, MU, TALL, WIDE), BF16), jax.ShapeDtypeStruct((MU, NU, TALL, 2 * SIDE), BF16)),
        in_specs=[VMEM, VMEM],
        out_specs=(VMEM, VMEM),
        scratch_shapes=[dma((CHUNKS,)), dma((MU, PA)), dma((PA, MU)), dma, dma((4,)), dma((4,)), dma((4, 4)), dma((4, 4)),
                        dma((4,)), dma((4,)), dma((4,)), dma((4,))],
        compiler_params=pltpu.CompilerParams(collective_id=1, has_side_effects=True, vmem_limit_bytes=LIMIT),
    )(block, density)


def sides_kernel(got, den, vt_ref, occ_ref, lhs, wide, turned):
    rows = got[...].reshape(PA * MU * TALL, WIDE)
    lane = lax.broadcasted_iota(jnp.int32, (PA, MU // 2, TALL, 128), 3)
    for p in range(SLAB):
        first = ROWS * p // 128 * 128
        span = min(256, WIDE - first)
        r, c = iotas((span, 128))
        atom, i = (c % 64) // TALL, c % TALL
        pick = one_hot((r == ROWS * p - first + atom * BAS + i) & (i < BAS))
        part = nn(rows[:, first:first + span], pick).astype(BF16).reshape(PA, MU // 2, 2, TALL, 128)
        both = jnp.where(lane < 64, part[:, :, 0], part[:, :, 1])
        for x in range(PA):
            for k in range(MU // 2):
                lhs[(x * SLAB + p) * TALL:(x * SLAB + p + 1) * TALL, k * 128:(k + 1) * 128] = both[x, k]
    eye_r, eye_c = iotas((SIDE, SIDE))
    eye = one_hot(eye_r == eye_c)
    density = den[...].reshape(DEPTH, 2 * SIDE)
    virt = nn(lhs[...], density[:, SIDE:]).astype(BF16)
    vt_ref[...] = nt(eye, virt).astype(BF16)
    occ = nn(lhs[...], density[:, :SIDE]).astype(BF16)
    occ_t = nt(eye, occ).astype(BF16)
    r, c = iotas((LINES, 128))
    p = r // TALL
    moved = p + (BLOCK - SLAB) * ((p >= SLAB).astype(jnp.int32) + (p >= 2 * SLAB) + (p >= 3 * SLAB))
    same = moved == c
    for n in range(TALL):
        wide[...] = nn(occ_t, one_hot(same & (r % TALL == n)))
        for l in range(TALL):
            turned[l, pl.ds(n, MU, stride=TALL), :] = wide[pl.ds(l, MU, stride=TALL), :]
    small_r, small_c = iotas((128, 128))
    small = one_hot(small_r == small_c)
    for l in range(TALL):
        occ_ref[l] = nt(small, turned[l].astype(BF16)).astype(BF16)


def sides(got, den):
    return pl.pallas_call(
        sides_kernel,
        out_shape=(jax.ShapeDtypeStruct((SIDE, LINES), BF16), jax.ShapeDtypeStruct((TALL, 128, SIDE), BF16)),
        in_specs=[VMEM, VMEM],
        out_specs=(VMEM, VMEM),
        scratch_shapes=[pltpu.VMEM((LINES, DEPTH), BF16), pltpu.VMEM((SIDE, 128), F32), pltpu.VMEM((TALL, SIDE, 128), F32)],
        compiler_params=pltpu.CompilerParams(vmem_limit_bytes=LIMIT),
    )(got, den)


def stages():
    pa, mu, nu = lax.axis_index("pa"), lax.axis_index("mu"), lax.axis_index("nu")
    y_lo, z = mu // DEEP, mu % DEEP
    slabs = (4, pa, lambda i: (i, mu, nu))
    plane = (8, y_lo * 4 + nu, lambda i: (pa, (i // 4) * DEEP + z, i % 4))
    near = (4, z % 4, lambda i: (pa, y_lo * DEEP + (z // 4) * 4 + i, nu))
    far = (4, z // 4, lambda i: (pa, y_lo * DEEP + i * 4 + z % 4, nu))
    return slabs, plane, near, far


def close_kernel(vt_ref, occ_ref, o_ref, virt, chi, acc, got0, got1, got2, got3, v_send, v_recv, own_sem, send_sem, recv_sem):
    pa, mu, nu, works, chunk = place()
    steps = stages()
    barrier = pltpu.get_barrier_semaphore()

    def greet(device):
        pl.semaphore_signal(barrier, inc=1, device_id=device, device_id_type=MESH)

    for size, me, at in steps:
        for d in range(1, size):
            greet(at((me + d) % size))

    @pl.when(works)
    def _():
        @pl.when(pa != nu)
        def _():
            greet((nu, mu, pa))

        @pl.loop(1, CHUNKS)
        def _(d):
            greet((nu, chunk_mu((chunk + d) % CHUNKS), pa))

    swaps = CHUNKS - 1 + (pa != nu).astype(jnp.int32)
    pl.semaphore_wait(barrier, 3 + 7 + 3 + 3 + jnp.where(works, swaps, 0))

    def part(j):
        return vt_ref.at[pl.ds(pl.multiple_of(j * TALL, TALL), TALL), :]

    def slot(j):
        return virt.at[pl.ds(pl.multiple_of(j * TALL, TALL), TALL), :]

    def swap(d):
        j = (chunk + d) % CHUNKS
        return remote(part(j), slot(chunk), v_send.at[d], v_recv.at[chunk], (nu, chunk_mu(j), pa))

    def swap_got(j):
        return remote(part(0), slot(j), v_send.at[0], v_recv.at[j], (nu, chunk_mu(j), pa))

    def mine():
        return pltpu.make_async_copy(part(chunk), slot(chunk), own_sem)

    @pl.when(works)
    def _():
        @pl.when(pa == nu)
        def _():
            mine().start()

        @pl.when(pa != nu)
        def _():
            swap(0).start()

        @pl.loop(1, CHUNKS)
        def _(d):
            swap(d).start()

        virt[COLS:, :] = jnp.zeros((SIDE - COLS, LINES), BF16)

        @pl.when(pa == nu)
        def _():
            mine().wait()

        @pl.when(pa != nu)
        def _():
            swap_got(chunk).wait_recv()

        @pl.loop(1, CHUNKS)
        def _(d):
            swap_got((chunk + d) % CHUNKS).wait_recv()

        lane = lax.broadcasted_iota(jnp.int32, (128, LINES), 1) % TALL
        total = jnp.zeros((128, LINES), F32)
        for l in range(TALL):
            total = jnp.where(lane == l, nn(occ_ref[l], virt[...]), total)
        r, c = iotas((LINES, 128))
        gather = jnp.where(r // TALL == c, 1.0, 0.0)
        chi[...] = jnp.dot(total, gather, precision=lax.Precision.HIGHEST, preferred_element_type=F32)

    @pl.when(jnp.logical_not(works))
    def _():
        chi[...] = jnp.zeros_like(chi)

    for s, ((size, me, at), got) in enumerate(zip(steps, (got0, got1, got2, got3))):
        def source(to):
            return chi.at[pl.ds(pl.multiple_of(to * BLOCK, 8), BLOCK), :] if s == 0 else acc

        for d in range(1, size):
            to = (me + d) % size
            remote(source(to), got.at[me], send_sem.at[s, d], recv_sem.at[s, me], at(to)).start()
        got[me] = source(me)[...]
        for d in range(1, size):
            frm = (me + d) % size
            remote(source(frm), got.at[frm], send_sem.at[s, d], recv_sem.at[s, frm], at(frm)).wait_recv()
        total = got[0]
        for i in range(1, size):
            total = total + got[i]
        for d in range(1, size):
            to = (me + d) % size
            remote(source(to), got.at[me], send_sem.at[s, d], recv_sem.at[s, me], at(to)).wait_send()
        acc[...] = total
    o_ref[...] = acc[:SLAB, :RI] / F32(NU * COLS)

    @pl.when(works)
    def _():
        @pl.when(pa != nu)
        def _():
            swap(0).wait_send()

        @pl.loop(1, CHUNKS)
        def _(d):
            swap(d).wait_send()


def close(vt, occ):
    dma = pltpu.SemaphoreType.DMA
    small = (BLOCK, 128)
    return pl.pallas_call(
        close_kernel,
        out_shape=jax.ShapeDtypeStruct((SLAB, RI), F32),
        in_specs=[VMEM, VMEM],
        out_specs=VMEM,
        scratch_shapes=[
            pltpu.VMEM((SIDE, LINES), BF16),
            pltpu.VMEM((128, 128), F32),
            pltpu.VMEM(small, F32),
            pltpu.VMEM((4,) + small, F32),
            pltpu.VMEM((8,) + small, F32),
            pltpu.VMEM((4,) + small, F32),
            pltpu.VMEM((4,) + small, F32),
            dma((CHUNKS,)), dma((CHUNKS,)), dma, dma((4, 8)), dma((4, 8)),
        ],
        compiler_params=pltpu.CompilerParams(collective_id=2, has_side_effects=True, vmem_limit_bytes=LIMIT),
    )(vt, occ)


def local(integrals, pattern, occ_density, virt_density):
    start = lax.axis_index("pa") * COLS

    def columns(density):
        return jnp.pad(lax.dynamic_slice_in_dim(density, start, COLS, 1), ((0, TALL - BAS), (0, SIDE - COLS)))

    density = jnp.concatenate([columns(occ_density), columns(virt_density)], axis=1)
    got, den = spread(turn(integrals, pattern), density)
    return close(*sides(got, den))


def solution(mesh):
    placed = (P("pa", "mu", "nu"), P("mu", "nu"), P(("mu", "nu"), None), P(("mu", "nu"), None))
    return jax.shard_map(
        local, mesh=mesh, in_specs=placed, out_specs=P("pa", None), check_vma=False
    )
```

time: 1090 us -> 243 us (0.22); the launches traced: 1070 us -> 242 us
  blocking collectives: 653 us -> 0 us
  waiting for transfers between devices: 261 us -> 0 us
  Pallas kernels: 0 us -> 240 us
  local copies, waits for them, and re-layouts: 131 us -> 2.13 us
  matrix products: 13.3 us -> 0 us
  between operations: 13.2 us -> 0.02 us
    psum x1 -> x0, blocking collectives: 492 us -> none  [local(): summed = lax.psum(block, ('mu', 'nu'))]
    all_gather x3 -> x0, waiting for transfers between devices: 259 us -> none  [the longest x1 166 us: local(): lax.all_gather(virt_density, ('mu', 'nu'), axis=0, tiled=True)]
    pallas_call x0 -> x4, Pallas kernels: none -> 240 us  [the longest x1 132 us: spread(): pl.pallas_call(spread_kernel, out_shape=(jax.ShapeDtypeStruct((PA, MU, TA...]
    all_to_all x2 -> x0, blocking collectives: 160 us -> none  [the longest x1 100 us: local(): lax.all_to_all(complete_input, ('mu', 'nu'), split_axis=1, concat_axis=1,...]
    reshape x6 -> x0, local copies, waits for them, and re-layouts: 95.3 us -> none  [the longest x2 34.5 us: local(): turned = jnp.transpose(moved, (0, 4, 2, 1, 3)).reshape(width, slab, basis)]
    unnamed x5 -> x1, local copies, waits for them, and re-layouts: 28.4 us -> 1.31 us
    dot_general x2 -> x0, matrix products: 13.3 us -> none  [the longest x1 8.56 us: local(): jnp.einsum('jpl,jql->pq', occ_side, lax.all_gather(turned, 'pa', axis=1,...]
  transfers between devices with their start and end apart: 3 -> 0, of which waited for: 3 -> 0; matrix products, arithmetic and copies ran while one was open for 12% -> 0% of each run, Pallas kernels for 0% -> 0%
where the time goes in v2:
time: 243 us; the launch traced here: 242 us
  Pallas kernels  240 us (99%)
    pallas_call x1, Pallas kernels, spread(): pl.pallas_call(spread_kernel, out_shape=(jax.ShapeDtypeStruct((PA, MU, TA...  132 us
    pallas_call x1, Pallas kernels, close(): pl.pallas_call(close_kernel, out_shape=jax.ShapeDtypeStruct((SLAB, RI), F...  77.3 us
    pallas_call x1, Pallas kernels, sides(): pl.pallas_call(sides_kernel, out_shape=(jax.ShapeDtypeStruct((SIDE, LINES...  25.5 us
    pallas_call x1, Pallas kernels, turn(): pl.pallas_call(turn_kernel, out_shape=jax.ShapeDtypeStruct((COLS, WIDE),...  4.87 us

profile of v2, /device:TPU:1, one launch (start us, length us, event | category | flops | bytes accessed | tf_op | source)
XLA Modules:
  0.0 242.3 jit_solution(17666014783822870121)
XLA Ops:
  0.0 0.8 constant_dynamic-slice_fusion
  0.8 0.6 fusion.2.d_ref
  1.4 4.9 %shard_map.46.b_ref = bf16[416,1152]{1,0:T(8,128)(2,1)} custom-call(bf16[20,52,416]{2,1,0:T(8,128)(2,1)} %m_ref.1, s32[4,32]{1,0:T(4,128)} %pat_ref.1), custom_call_target="tpu_custom_call" | custom-call | tf_op jit(solution)/shard_map/pallas_call | solution.py:81
  6.3 131.8 %shard_map.47 = (bf16[4,32,16,1152]{3,2,1,0:T(8,128)(2,1)}, bf16[32,4,16,1024]{3,2,1,0:T(8,128)(2,1)}) custom-call(bf16[416,1152]{1,0:T(8,128)(2,1)} %shard_map.46.b_ref, bf16[16,1024]{1,0:T(8,128)(2,1)} %fusion.2.d_ref), custom_call_target="tpu_custom_call" | custom-call | tf_op jit(solution)/shard_map/pallas_call | solution.py:247
  138.1 25.5 %shard_map.48 = (bf16[512,1280]{1,0:T(8,128)(2,1)}, bf16[16,128,512]{2,1,0:T(8,128)(2,1)}) custom-call(bf16[4,32,16,1152]{3,2,1,0:T(8,128)(2,1)} %get-tuple-element.9.got, bf16[32,4,16,1024]{3,2,1,0:T(8,128)(2,1)} %get-tuple-element.10.den), custom_call_target="tpu_custom_call" | custom-call | tf_op jit(solution)/shard_map/pallas_call | solution.py:294
  163.6 77.3 %shard_map.49 = f32[20,80]{1,0:T(8,128)} custom-call(bf16[512,1280]{1,0:T(8,128)(2,1)} %get-tuple-element.11.vt_ref, bf16[16,128,512]{2,1,0:T(8,128)(2,1)} %get-tuple-element.12.occ_ref), custom_call_target="tpu_custom_call" | custom-call | tf_op jit(solution)/shard_map/pallas_call | solution.py:429
  241.0 1.3 copy.6

commit v3 on v0

v3 whole, which is shorter than its diff:
```python
import functools

import jax
import jax.numpy as jnp
from jax import lax
from jax.experimental import pallas as pl
from jax.experimental.pallas import tpu as pltpu
from jax.sharding import PartitionSpec as P

MESH = pl.DeviceIdType.MESH
F32, BF16 = jnp.float32, jnp.bfloat16
PA, MU, NU, DEEP = 4, 32, 4, 16
BAS, TALL = 13, 16
SLAB, ROWS, COLS = 20, 52, 416
RI = PA * SLAB
CHUNKS = COLS // TALL
HALF = CHUNKS // 2
WIDE = 1152
BOTH = 896
EVEN = 384
SIDE = 512
LINES = RI * TALL
DEPTH = MU * NU * TALL
LAG = 4
AHEAD = 8
BLOCK = 24
VMEM = pl.BlockSpec(memory_space=pltpu.VMEM)
LIMIT = 56 * 1024 * 1024


def nt(a, b):
    return lax.dot_general(a, b, (((1,), (1,)), ((), ())), preferred_element_type=F32)


def nn(a, b):
    return jnp.dot(a, b, preferred_element_type=F32)


def iotas(shape):
    return lax.broadcasted_iota(jnp.int32, shape, 0), lax.broadcasted_iota(jnp.int32, shape, 1)


def one_hot(where):
    return jnp.where(where, 1.0, 0.0).astype(BF16)


def place():
    pa, mu, nu = lax.axis_index("pa"), lax.axis_index("mu"), lax.axis_index("nu")
    z = mu % DEEP
    return pa, mu, nu, z % 5 != 4, (mu // DEEP) * HALF + z - z // 5


def chunk_mu(chunk):
    r = chunk % HALF
    return (chunk // HALF) * DEEP + r + r // 4


def remote(src, dst, send, recv, device):
    return pltpu.make_async_remote_copy(
        src_ref=src, dst_ref=dst, send_sem=send, recv_sem=recv, device_id=device, device_id_type=MESH)


def stages():
    pa, mu, nu = lax.axis_index("pa"), lax.axis_index("mu"), lax.axis_index("nu")
    y_lo, z = mu // DEEP, mu % DEEP
    slabs = (4, pa, lambda i: (i, mu, nu))
    plane = (8, y_lo * 4 + nu, lambda i: (pa, (i // 4) * DEEP + z, i % 4))
    near = (4, z % 4, lambda i: (pa, y_lo * DEEP + (z // 4) * 4 + i, nu))
    far = (4, z // 4, lambda i: (pa, y_lo * DEEP + i * 4 + z % 4, nu))
    return slabs, plane, near, far


def response_kernel(m_ref, pat_ref, d_ref, o_ref, held, block, got, den, lhs, picks, eye, vt, virt, wide, turned, occ, chi, acc,
                    got0, got1, got2, got3, mu_send, fwd_send, got_recv, own_sem, ring_send, ring_recv,
                    y_send, y_recv, core_send, core_recv, v_send, v_recv, mine_sem, sum_send, sum_recv):
    pa, mu, nu, works, chunk = place()
    idle = jnp.logical_not(works)
    y_lo, z, y_hi, core = mu // DEEP, mu % DEEP, nu // 2, nu % 2
    y = y_hi * 2 + y_lo
    right, left, across_pa = (pa + 1) % PA, (pa + 3) % PA, (pa + 2) % PA
    mate = (pa, mu, y_hi * 2 + 1 - core)

    def at_y(other):
        return (pa, (other % 2) * DEEP + z, (other // 2) * 2 + core)

    barrier = pltpu.get_barrier_semaphore()

    def greet(device):
        pl.semaphore_signal(barrier, inc=1, device_id=device, device_id_type=MESH)

    @pl.loop(1, MU)
    def _(d):
        greet((pa, (mu + d) % MU, nu))

    for d in range(1, PA):
        greet(((pa + d) % PA, mu, nu))
        greet((pa, mu, (nu + d) % NU))
        greet((pa, (1 - y_lo) * DEEP + z, (nu + d) % NU))

    @pl.when(works)
    def _():
        @pl.when(pa != nu)
        def _():
            greet((nu, mu, pa))

        @pl.loop(1, CHUNKS)
        def _(d):
            greet((nu, chunk_mu((chunk + d) % CHUNKS), pa))

    den[mu, nu] = d_ref[...]
    r, c = iotas((64, 4))
    spread_m = one_hot((r >= c * BAS) & (r < c * BAS + BAS))
    r, c = iotas((32, COLS))
    spread_n = one_hot((c >= r * BAS) & (c < r * BAS + BAS))
    pat = nn(spread_m, pat_ref[...].astype(F32).astype(BF16))
    mask = nn(pat.astype(BF16), spread_n)[:ROWS]
    held[...] = jnp.zeros_like(held)
    for p in range(SLAB):
        held[p, :ROWS, :] = (m_ref[p].astype(F32) * mask).astype(BF16)
    r, c = iotas((SIDE, SIDE))
    eye[...] = one_hot(r == c)
    r, c = iotas((WIDE, 256))
    dense = jnp.zeros((WIDE, COLS), F32)
    for g in range(SLAB // 4):
        p, m = 4 * g + c // 64, c % 64
        pick = one_hot((r == p * ROWS + m) & (m < ROWS))
        dense = dense + nn(pick, held[4 * g:4 * g + 4].reshape(256, COLS))
    block[...] = nt(eye[:COLS, :COLS], dense.astype(BF16)).astype(BF16)

    swaps = CHUNKS - 1 + (pa != nu).astype(jnp.int32)
    pl.semaphore_wait(barrier, MU - 1 + 3 * (PA - 1) + jnp.where(works, swaps, 0))

    def ring(t, way):
        src = den.at[y_lo * DEEP + (z + (DEEP - t if way == 0 else t)) % DEEP, nu]
        to = (pa, y_lo * DEEP + (z + (1 if way == 0 else DEEP - 1)) % DEEP, nu)
        return remote(src, src, ring_send.at[way, t], ring_recv.at[(z + (DEEP - t if way == 0 else t)) % DEEP], to)

    ring(0, 0).start()
    ring(0, 1).start()

    def ring_step(t):
        ring(t, 0).wait_recv()

        @pl.when(t < DEEP // 2)
        def _():
            ring(t, 0).start()
            ring(t, 1).wait_recv()

        @pl.when(t < DEEP // 2 - 1)
        def _():
            ring(t, 1).start()

    def across(d):
        j = (chunk + d) % CHUNKS
        src = block.at[pl.ds(pl.multiple_of(j * TALL, TALL), TALL), :]
        return remote(src, got.at[pa, mu], mu_send.at[d], got_recv.at[pa, mu], (pa, chunk_mu(j), nu))

    def own():
        src = block.at[pl.ds(pl.multiple_of(chunk * TALL, TALL), TALL), :]
        return pltpu.make_async_copy(src, got.at[pa, mu], own_sem)

    @pl.when(works)
    def _():
        own().start()

    @pl.when(idle)
    def _():
        across(0).start()

    @pl.loop(1, AHEAD)
    def _(d):
        across(d).start()

    for p in range(SLAB):
        first = ROWS * p // 128 * 128
        r, c = iotas((256, 128))
        atom, i = (c % 64) // TALL, c % TALL
        picks[p] = one_hot((r == ROWS * p - first + atom * BAS + i) & (i < BAS))

    def slot(x, k):
        return remote(got.at[x, k], got.at[x, k], mu_send.at[0], got_recv.at[x, k], mate)

    def forward(x, k, s, to):
        return remote(got.at[x, k], got.at[x, k], fwd_send.at[k, s], got_recv.at[x, k], (to, mu, nu))

    def source(e):
        return (mu + MU - e) % MU

    def beyond(e):
        odd = e % 2
        return forward((pa + 3 + 2 * odd) % PA, source(e), 2, (pa + 1 + 2 * odd) % PA)

    def both_ways(k):
        forward(pa, k, 0, right).start()
        forward(pa, k, 1, left).start()

    def advance(e):
        @pl.when(e + AHEAD <= CHUNKS)
        def _():
            across(e + AHEAD - 1).start()

        @pl.when((e % 2 == 0) & (e <= DEEP))
        def _():
            ring_step(e // 2)

    def pass_beyond(low, high):
        @pl.loop(low, high)
        def _(e):
            slot(right, source(e)).wait_recv()
            slot(left, source(e)).wait_recv()
            beyond(e).start()

    def pass_all(low, high):
        @pl.loop(low, high)
        def _(e):
            advance(e)

            @pl.when(works)
            def _():
                slot(pa, source(e)).wait_recv()
                both_ways(source(e))

                @pl.when(e >= LAG)
                def _():
                    slot(right, source(e - LAG)).wait_recv()
                    slot(left, source(e - LAG)).wait_recv()
                    beyond(e - LAG).start()

    @pl.when(works)
    def _():
        own().wait()
        both_ways(mu)

    pass_all(1, DEEP + 1)

    def plane(other, half, side):
        return den.at[pl.ds((other % 2) * DEEP + half * 8, 8), (other // 2) * 2 + side]

    def over_y(other, half, s, to):
        src = plane(other, half, core)
        return remote(src, src, y_send.at[s, half], y_recv.at[other, half], at_y(to))

    def y_wait(other, half):
        src = plane(other, half, core)
        remote(src, src, y_send.at[0, 0], y_recv.at[other, half], mate).wait_recv()

    def to_mate(other, half):
        src = plane(other, half, core)
        return remote(src, src, core_send.at[other, half], core_recv.at[other, half], mate)

    def mate_wait(other, half):
        src = plane(other, half, 1 - core)
        remote(src, src, core_send.at[0, 0], core_recv.at[other, half], mate).wait_recv()

    up, down, over = (y + 1) % 4, (y + 3) % 4, (y + 2) % 4

    @pl.when(works)
    def _():
        for half in range(2):
            over_y(y, half, 0, up).start()
            over_y(y, 1 - half, 1, down).start()
        for half in range(2):
            to_mate(y, half).start()

    pass_all(DEEP + 1, 22)

    @pl.when(works)
    def _():
        y_wait(down, 0)
        over_y(down, 0, 2, up).start()
        y_wait(up, 1)
        over_y(up, 1, 2, down).start()
        to_mate(down, 0).start()
        to_mate(up, 1).start()

    pass_all(22, 27)

    @pl.when(works)
    def _():
        y_wait(down, 1)
        y_wait(up, 0)
        to_mate(down, 1).start()
        to_mate(up, 0).start()

    pass_all(27, MU)

    def part(j, half):
        return vt.at[half, pl.ds(pl.multiple_of(j * TALL, TALL), TALL), :]

    def place_of(j, half):
        return virt.at[half, pl.ds(pl.multiple_of(j * TALL, TALL), TALL), :]

    def swap(d, half):
        j = (chunk + d) % CHUNKS
        return remote(part(j, half), place_of(chunk, half), v_send.at[half, d], v_recv.at[half, chunk], (nu, chunk_mu(j), pa))

    def swap_got(j, half):
        return remote(part(0, half), place_of(j, half), v_send.at[0, 0], v_recv.at[half, j], mate)

    def mine(half):
        return pltpu.make_async_copy(part(chunk, half), place_of(chunk, half), mine_sem.at[half])

    def swap_start(half):
        @pl.when(pa == nu)
        def _():
            mine(half).start()

        @pl.when(pa != nu)
        def _():
            swap(0, half).start()

        @pl.loop(1, CHUNKS)
        def _(d):
            swap(d, half).start()

    def swap_wait(half):
        @pl.when(pa == nu)
        def _():
            mine(half).wait()

        @pl.when(pa != nu)
        def _():
            swap_got(chunk, half).wait_recv()

        @pl.loop(1, CHUNKS)
        def _(d):
            swap_got((chunk + d) % CHUNKS, half).wait_recv()

    @pl.when(works)
    def _():
        lane = lax.broadcasted_iota(jnp.int32, (MU // 2, TALL, 128), 2)

        def unpack(e, x):
            for p in range(SLAB):
                first = ROWS * p // 128 * 128
                rows = got[x, :, :, first:first + 256].reshape(MU * TALL, 256)
                part = nn(rows, picks[p]).astype(BF16).reshape(MU // 2, 2, TALL, 128)
                both = jnp.where(lane < 64, part[:, 0], part[:, 1])
                for k in range(MU // 2):
                    lhs[(e * SLAB + p) * TALL:(e * SLAB + p + 1) * TALL, k * 128:(k + 1) * 128] = both[k]

        shift_r, shift_c = iotas((SIDE, SIDE))
        shift = one_hot((shift_c == shift_r + COLS - EVEN) & (shift_r < COLS))

        def virtual(half):
            rows = lhs[half * (LINES // 2):(half + 1) * (LINES // 2), :]
            lines = nn(rows, den[:, :, :, EVEN:].reshape(DEPTH, SIDE)).astype(BF16)
            vt[half] = nt(shift, lines).astype(BF16)
            swap_start(half)

        unpack(0, pa)
        pass_beyond(MU - LAG, MU)
        for half in range(2):
            y_wait(over, half)
            to_mate(over, half).start()
        unpack(1, right)
        for other in range(4):
            for half in range(2):
                mate_wait(other, half)
        virtual(0)
        unpack(2, left)

        @pl.loop(0, MU)
        def _(k):
            slot(across_pa, k).wait_recv()

        unpack(3, across_pa)
        virtual(1)

        virt[:, COLS:, :] = jnp.zeros((2, SIDE - COLS, LINES // 2), BF16)
        lines = nn(lhs[...], den[:, :, :, :SIDE].reshape(DEPTH, SIDE)).astype(BF16)
        lines = nt(eye[...], lines).astype(BF16)
        r, c = iotas((LINES, 128))
        turn_of = r // (SLAB * TALL)
        slab_of = (pa + jnp.where(turn_of >= 2, 5 - turn_of, turn_of)) % PA
        same = slab_of * BLOCK + (r // TALL) % SLAB == c
        for n in range(TALL):
            wide[...] = nn(lines, one_hot(same & (r % TALL == n)))
            for l in range(TALL):
                turned[l, pl.ds(n, MU, stride=TALL), :] = wide[pl.ds(l, MU, stride=TALL), :]
        for l in range(TALL):
            occ[l] = nt(eye[:128, :128], turned[l].astype(BF16)).astype(BF16)

        r, c = iotas((LINES // 2, 128))
        lane = lax.broadcasted_iota(jnp.int32, (128, LINES // 2), 1) % TALL
        result = jnp.zeros((128, 128), F32)
        for half in range(2):
            swap_wait(half)
            total = jnp.zeros((128, LINES // 2), F32)
            for l in range(TALL):
                total = jnp.where(lane == l, nn(occ[l], virt[half]), total)
            turn_of = r // (SLAB * TALL) + 2 * half
            slab_of = (nu + jnp.where(turn_of >= 2, 5 - turn_of, turn_of)) % PA
            gather = jnp.where(slab_of * SLAB + (r // TALL) % SLAB == c, 1.0, 0.0)
            result = result + jnp.dot(total, gather, precision=lax.Precision.HIGHEST, preferred_element_type=F32)
        chi[...] = result

    @pl.when(idle)
    def _():
        chi[...] = jnp.zeros_like(chi)

    for s, ((size, me, at), kept) in enumerate(zip(stages(), (got0, got1, got2, got3))):
        def share(to):
            return chi.at[pl.ds(pl.multiple_of(to * BLOCK, 8), BLOCK), :] if s == 0 else acc

        def send(to, d):
            return remote(share(to), kept.at[me], sum_send.at[s, d], sum_recv.at[s, me], at(to))

        for d in range(1, size):
            send((me + d) % size, d).start()
        kept[me] = share(me)[...]
        for d in range(1, size):
            frm = (me + d) % size
            remote(share(frm), kept.at[frm], sum_send.at[s, d], sum_recv.at[s, frm], at(frm)).wait_recv()
        total = kept[0]
        for i in range(1, size):
            total = total + kept[i]
        for d in range(1, size):
            send((me + d) % size, d).wait_send()
        acc[...] = total
    o_ref[...] = acc[:SLAB, :RI] / F32(NU * COLS)

    for t in range(DEEP // 2):
        ring(t, 0).wait_send()
        if t < DEEP // 2 - 1:
            ring(t, 1).wait_send()

    @pl.when(idle)
    def _():
        across(0).wait_send()

    @pl.loop(1, CHUNKS)
    def _(d):
        across(d).wait_send()

    @pl.when(works)
    def _():
        @pl.loop(0, MU)
        def _(e):
            forward(pa, source(e), 0, right).wait_send()
            forward(pa, source(e), 1, left).wait_send()
            beyond(e).wait_send()

        for half in range(2):
            over_y(y, half, 0, up).wait_send()
            over_y(y, half, 1, down).wait_send()
            for other in range(4):
                to_mate(other, half).wait_send()
        over_y(down, 0, 2, up).wait_send()
        over_y(up, 1, 2, down).wait_send()

        for half in range(2):
            @pl.when(pa != nu)
            def _():
                swap(0, half).wait_send()

            @pl.loop(1, CHUNKS)
            def _(d):
                swap(d, half).wait_send()


def response(integrals, pattern, density):
    dma = pltpu.SemaphoreType.DMA
    small = (BLOCK, 128)
    return pl.pallas_call(
        response_kernel,
        out_shape=jax.ShapeDtypeStruct((SLAB, RI), F32),
        in_specs=[VMEM, VMEM, VMEM],
        out_specs=VMEM,
        scratch_shapes=[
            pltpu.VMEM((SLAB, 64, COLS), BF16),
            pltpu.VMEM((COLS, WIDE), BF16),
            pltpu.VMEM((PA, MU, TALL, WIDE), BF16),
            pltpu.VMEM((MU, NU, TALL, BOTH), BF16),
            pltpu.VMEM((LINES, DEPTH), BF16),
            pltpu.VMEM((SLAB, 256, 128), BF16),
            pltpu.VMEM((SIDE, SIDE), BF16),
            pltpu.VMEM((2, SIDE, LINES // 2), BF16),
            pltpu.VMEM((2, SIDE, LINES // 2), BF16),
            pltpu.VMEM((SIDE, 128), F32),
            pltpu.VMEM((TALL, SIDE, 128), F32),
            pltpu.VMEM((TALL, 128, SIDE), BF16),
            pltpu.VMEM((128, 128), F32),
            pltpu.VMEM(small, F32),
            pltpu.VMEM((4,) + small, F32),
            pltpu.VMEM((8,) + small, F32),
            pltpu.VMEM((4,) + small, F32),
            pltpu.VMEM((4,) + small, F32),
            dma((CHUNKS,)), dma((MU, 3)), dma((PA, MU)), dma, dma((2, 9)), dma((DEEP,)),
            dma((3, 2)), dma((4, 2)), dma((4, 2)), dma((4, 2)), dma((2, CHUNKS)), dma((2, CHUNKS)), dma((2,)), dma((4, 8)), dma((4, 8)),
        ],
        compiler_params=pltpu.CompilerParams(collective_id=1, has_side_effects=True, vmem_limit_bytes=LIMIT),
    )(integrals, pattern, density)


def local(integrals, pattern, occ_density, virt_density):
    start = lax.axis_index("pa") * COLS

    both = jnp.concatenate([lax.dynamic_slice_in_dim(d, start, COLS, 1) for d in (occ_density, virt_density)], axis=1)
    density = jnp.pad(both, ((0, TALL - BAS), (0, BOTH - 2 * COLS)))
    return response(integrals, pattern, density)


def solution(mesh):
    placed = (P("pa", "mu", "nu"), P("mu", "nu"), P(("mu", "nu"), None), P(("mu", "nu"), None))
    return jax.shard_map(
        local, mesh=mesh, in_specs=placed, out_specs=P("pa", None), check_vma=False
    )
```

time: 1090 us -> 174 us (0.16); the launches traced: 1070 us -> 173 us
  blocking collectives: 653 us -> 0 us
  waiting for transfers between devices: 261 us -> 0 us
  Pallas kernels: 0 us -> 170 us
  local copies, waits for them, and re-layouts: 131 us -> 2.13 us
  matrix products: 13.3 us -> 0 us
  between operations: 13.2 us -> 0.01 us
    psum x1 -> x0, blocking collectives: 492 us -> none  [local(): summed = lax.psum(block, ('mu', 'nu'))]
    all_gather x3 -> x0, waiting for transfers between devices: 259 us -> none  [the longest x1 166 us: local(): lax.all_gather(virt_density, ('mu', 'nu'), axis=0, tiled=True)]
    pallas_call x0 -> x1, Pallas kernels: none -> 170 us  [response(): pl.pallas_call(response_kernel, out_shape=jax.ShapeDtypeStruct((SLAB, RI)...]
    all_to_all x2 -> x0, blocking collectives: 160 us -> none  [the longest x1 100 us: local(): lax.all_to_all(complete_input, ('mu', 'nu'), split_axis=1, concat_axis=1,...]
    reshape x6 -> x0, local copies, waits for them, and re-layouts: 95.3 us -> none  [the longest x2 34.5 us: local(): turned = jnp.transpose(moved, (0, 4, 2, 1, 3)).reshape(width, slab, basis)]
    unnamed x5 -> x1, local copies, waits for them, and re-layouts: 28.4 us -> 1.31 us
    dot_general x2 -> x0, matrix products: 13.3 us -> none  [the longest x1 8.56 us: local(): jnp.einsum('jpl,jql->pq', occ_side, lax.all_gather(turned, 'pa', axis=1,...]
  transfers between devices with their start and end apart: 3 -> 0, of which waited for: 3 -> 0; matrix products, arithmetic and copies ran while one was open for 12% -> 0% of each run, Pallas kernels for 0% -> 0%
where the time goes in v3:
time: 174 us; the launch traced here: 173 us
  Pallas kernels  170 us (98%)
  local copies, waits for them, and re-layouts  2.13 us (1%)
    pallas_call x1, Pallas kernels, response(): pl.pallas_call(response_kernel, out_shape=jax.ShapeDtypeStruct((SLAB, RI)...  170 us

profile of v3, /device:TPU:1, one launch (start us, length us, event | category | flops | bytes accessed | tf_op | source)
XLA Modules:
  0.0 172.9 jit_solution(13639309470099869034)
XLA Ops:
  0.0 0.8 constant_dynamic-slice_fusion
  0.8 0.7 fusion.5.d_ref
  1.5 170.1 %shard_map.46 = f32[20,80]{1,0:T(8,128)} custom-call(bf16[20,52,416]{2,1,0:T(8,128)(2,1)} %m_ref.1, s32[4,32]{1,0:T(4,128)} %pat_ref.1, bf16[16,896]{1,0:T(8,128)(2,1)} %fusion.5.d_ref), custom_call_target="tpu_custom_call" | custom-call | tf_op jit(solution)/shard_map/pallas_call | solution.py:465
  171.6 1.3 copy.6

commit v4 on v3

--- a/solution.py
+++ b/solution.py
@@ -55,6 +55,10 @@
     return (chunk // HALF) * DEEP + r + r // 4
 
 
+def sway(d):
+    return jnp.where(d % 2 == 1, (d + 1) // 2, -(d // 2))
+
+
 def remote(src, dst, send, recv, device):
     return pltpu.make_async_remote_copy(
         src_ref=src, dst_ref=dst, send_sem=send, recv_sem=recv, device_id=device, device_id_type=MESH)
@@ -63,15 +67,14 @@
 def stages():
     pa, mu, nu = lax.axis_index("pa"), lax.axis_index("mu"), lax.axis_index("nu")
     y_lo, z = mu // DEEP, mu % DEEP
-    slabs = (4, pa, lambda i: (i, mu, nu))
+    apart = (16, (z // 4) * 4 + pa, lambda i: (i % 4, y_lo * DEEP + (i // 4) * 4 + z % 4, nu))
     plane = (8, y_lo * 4 + nu, lambda i: (pa, (i // 4) * DEEP + z, i % 4))
     near = (4, z % 4, lambda i: (pa, y_lo * DEEP + (z // 4) * 4 + i, nu))
-    far = (4, z // 4, lambda i: (pa, y_lo * DEEP + i * 4 + z % 4, nu))
-    return slabs, plane, near, far
+    return apart, plane, near
 
 
 def response_kernel(m_ref, pat_ref, d_ref, o_ref, held, block, got, den, lhs, picks, eye, vt, virt, wide, turned, occ, chi, acc,
-                    got0, got1, got2, got3, mu_send, fwd_send, got_recv, own_sem, ring_send, ring_recv,
+                    got0, got1, got2, mu_send, fwd_send, got_recv, own_sem, ring_send, ring_recv,
                     y_send, y_recv, core_send, core_recv, v_send, v_recv, mine_sem, sum_send, sum_recv):
     pa, mu, nu, works, chunk = place()
     idle = jnp.logical_not(works)
@@ -92,10 +95,13 @@
     def _(d):
         greet((pa, (mu + d) % MU, nu))
 
+    for size, me, at in stages():
+        @pl.loop(1, size)
+        def _(d):
+            greet(at((me + d) % size))
+
     for d in range(1, PA):
         greet(((pa + d) % PA, mu, nu))
-        greet((pa, mu, (nu + d) % NU))
-        greet((pa, (1 - y_lo) * DEEP + z, (nu + d) % NU))
 
     @pl.when(works)
     def _():
@@ -128,7 +134,7 @@
     block[...] = nt(eye[:COLS, :COLS], dense.astype(BF16)).astype(BF16)
 
     swaps = CHUNKS - 1 + (pa != nu).astype(jnp.int32)
-    pl.semaphore_wait(barrier, MU - 1 + 3 * (PA - 1) + jnp.where(works, swaps, 0))
+    pl.semaphore_wait(barrier, MU - 1 + 15 + 7 + 3 + PA - 1 + jnp.where(works, swaps, 0))
 
     def ring(t, way):
         src = den.at[y_lo * DEEP + (z + (DEEP - t if way == 0 else t)) % DEEP, nu]
@@ -151,7 +157,7 @@
             ring(t, 1).start()
 
     def across(d):
-        j = (chunk + d) % CHUNKS
+        j = (chunk + CHUNKS + sway(d)) % CHUNKS
         src = block.at[pl.ds(pl.multiple_of(j * TALL, TALL), TALL), :]
         return remote(src, got.at[pa, mu], mu_send.at[d], got_recv.at[pa, mu], (pa, chunk_mu(j), nu))
 
@@ -184,7 +190,7 @@
         return remote(got.at[x, k], got.at[x, k], fwd_send.at[k, s], got_recv.at[x, k], (to, mu, nu))
 
     def source(e):
-        return (mu + MU - e) % MU
+        return (mu + MU - sway(e)) % MU
 
     def beyond(e):
         odd = e % 2
@@ -291,7 +297,7 @@
         return virt.at[half, pl.ds(pl.multiple_of(j * TALL, TALL), TALL), :]
 
     def swap(d, half):
-        j = (chunk + d) % CHUNKS
+        j = (chunk + CHUNKS + sway(d)) % CHUNKS
         return remote(part(j, half), place_of(chunk, half), v_send.at[half, d], v_recv.at[half, chunk], (nu, chunk_mu(j), pa))
 
     def swap_got(j, half):
@@ -399,24 +405,33 @@
     def _():
         chi[...] = jnp.zeros_like(chi)
 
-    for s, ((size, me, at), kept) in enumerate(zip(stages(), (got0, got1, got2, got3))):
+    for s, ((size, me, at), kept) in enumerate(zip(stages(), (got0, got1, got2))):
         def share(to):
-            return chi.at[pl.ds(pl.multiple_of(to * BLOCK, 8), BLOCK), :] if s == 0 else acc
-
-        def send(to, d):
+            return chi.at[pl.ds(pl.multiple_of((to % PA) * BLOCK, 8), BLOCK), :] if s == 0 else acc
+
+        def send(d):
+            to = (me + d) % size
             return remote(share(to), kept.at[me], sum_send.at[s, d], sum_recv.at[s, me], at(to))
 
-        for d in range(1, size):
-            send((me + d) % size, d).start()
+        @pl.loop(1, size)
+        def _(d):
+            send(d).start()
+
         kept[me] = share(me)[...]
-        for d in range(1, size):
+
+        @pl.loop(1, size)
+        def _(d):
             frm = (me + d) % size
-            remote(share(frm), kept.at[frm], sum_send.at[s, d], sum_recv.at[s, frm], at(frm)).wait_recv()
+            remote(share(frm), kept.at[frm], sum_send.at[s, d], sum_recv.at[s, frm], mate).wait_recv()
+
         total = kept[0]
         for i in range(1, size):
             total = total + kept[i]
-        for d in range(1, size):
-            send((me + d) % size, d).wait_send()
+
+        @pl.loop(1, size)
+        def _(d):
+            send(d).wait_send()
+
         acc[...] = total
     o_ref[...] = acc[:SLAB, :RI] / F32(NU * COLS)
 
@@ -482,12 +497,11 @@
             pltpu.VMEM((TALL, 128, SIDE), BF16),
             pltpu.VMEM((128, 128), F32),
             pltpu.VMEM(small, F32),
-            pltpu.VMEM((4,) + small, F32),
+            pltpu.VMEM((16,) + small, F32),
             pltpu.VMEM((8,) + small, F32),
             pltpu.VMEM((4,) + small, F32),
-            pltpu.VMEM((4,) + small, F32),
             dma((CHUNKS,)), dma((MU, 3)), dma((PA, MU)), dma, dma((2, 9)), dma((DEEP,)),
-            dma((3, 2)), dma((4, 2)), dma((4, 2)), dma((4, 2)), dma((2, CHUNKS)), dma((2, CHUNKS)), dma((2,)), dma((4, 8)), dma((4, 8)),
+            dma((3, 2)), dma((4, 2)), dma((4, 2)), dma((4, 2)), dma((2, CHUNKS)), dma((2, CHUNKS)), dma((2,)), dma((3, 16)), dma((3, 16)),
         ],
         compiler_params=pltpu.CompilerParams(collective_id=1, has_side_effects=True, vmem_limit_bytes=LIMIT),
     )(integrals, pattern, density)

time: 174 us -> 177 us (1.017)
  Pallas kernels: 170 us -> 173 us
    pallas_call x1, Pallas kernels: 170 us -> 173 us  [response(): pl.pallas_call(response_kernel, out_shape=jax.ShapeDtypeStruct((SLAB, RI)...]
where the time goes in v4:
time: 177 us; the launch traced here: 176 us
  Pallas kernels  173 us (98%)
  local copies, waits for them, and re-layouts  2.13 us (1%)
    pallas_call x1, Pallas kernels, response(): pl.pallas_call(response_kernel, out_shape=jax.ShapeDtypeStruct((SLAB, RI)...  173 us

profile of v4, /device:TPU:1, one launch (start us, length us, event | category | flops | bytes accessed | tf_op | source)
XLA Modules:
  0.0 175.7 jit_solution(6501286314747135433)
XLA Ops:
  0.0 0.8 constant_dynamic-slice_fusion
  0.8 0.7 fusion.5.d_ref
  1.5 172.9 %shard_map.46 = f32[20,80]{1,0:T(8,128)} custom-call(bf16[20,52,416]{2,1,0:T(8,128)(2,1)} %m_ref.1, s32[4,32]{1,0:T(4,128)} %pat_ref.1, bf16[16,896]{1,0:T(8,128)(2,1)} %fusion.5.d_ref), custom_call_target="tpu_custom_call" | custom-call | tf_op jit(solution)/shard_map/pallas_call | solution.py:480
  174.4 1.3 copy.6
